TPU v7x, 32 devices: a whole 2x2x4 slice. The times are simulated.
32 devices in a mesh: groups: 2 (over y), seq: 4 (over z), mp: 2 (over x), rep: 2 (over core).
Axes of the slice: x: 2, y: 2, z: 4, core: 2. Of those that a mesh axis runs over, the one named last changes fastest.
Arguments:
- tokens: bfloat16 [4, 2048, 1024], P(('groups', 'rep'), ('seq', 'mp')), parts along dimension 0, may hold values from -6 to 6
- w_qkv: bfloat16 [1024, 3, 1024], P(None, None, 'mp')
- w_attn_out: bfloat16 [1024, 1024], P('mp'), may hold values from -0.1875 to 0.1875
- w_in: bfloat16 [1024, 2624], P(None, 'mp'), may hold values from -0.1875 to 0.1875
- w_gate: bfloat16 [1024, 2624], P(None, 'mp'), may hold values from -0.1875 to 0.1875
- w_down: bfloat16 [1024, 2624], P(None, 'mp'), may hold values from -0.125 to 0.125
- w_colbert: bfloat16 [1024, 128], replicated, may hold values from -0.1875 to 0.1875
- gain_attn: float32 [1024], replicated, may hold values from 0.1 to 1.9
- gain_mlp: float32 [1024], replicated, may hold values from 0.1 to 1.9
- gain_final: float32 [1024], replicated, may hold values from 0.1 to 1.9
- lengths: int32 [4, 8], P(('groups', 'rep')), parts along dimension 0, may hold values from 1 to 1024, 2048 in all within a row
- owners: int32 [4, 2048, 1], P(('groups', 'rep'), ('seq', 'mp')), parts along dimension 0, may hold values from 0 to 15; in each aligned block of 256 rows (0 to 255, 256 to 511, ..., all dimensions but the last counted through in order) at most 32 rows name the same one
Outputs:
- routed: bfloat16 [512, 32, 128], P(('groups', 'seq', 'mp', 'rep')), parts along dimension 0
There are 2 independent parts, one for each index of `groups`. A program takes and returns all parts, laid end to end along the dimension named above; an argument that names none is the same for every part. Nothing has to cross between parts.
Inputs may be any that keep to these rules, and one draw needn't show every extreme that they name: The 8 lengths of a slab sum to 2048 and the longest is exactly 1024. `owners`: within the 256 positions of one device (aligned blocks of the slab-major order) no owner appears more than 32 times; in every draw some owner appears exactly 32 times in some block.
All inputs are finite; a program needn't handle non-finite values.
Results may differ from a plain program's by a relative error of at most 0.01.
Values may be sent and summed in bfloat16 or wider, within the bound.
A program may use at most 128 MiB of HBM per device.

v0:
```python
import jax
import jax.numpy as jnp
from jax import lax
from jax.sharding import PartitionSpec as P

HEAD_DIM = 64
WIN = 64


epsilon = 1e-05
rope_base = 10000.0


def with_halo(cells, sides, width):
    for axis, dim in sides:
        count = lax.axis_size(axis)
        ends = count - 1
        head = lax.slice_in_dim(cells, 0, width, axis=dim)
        tail = lax.slice_in_dim(cells, cells.shape[dim] - width, cells.shape[dim], axis=dim)
        cells = jnp.concatenate(
            [
                lax.ppermute(tail, axis, [(i, (i + 1) % count) for i in range(ends)]),
                cells,
                lax.ppermute(head, axis, [((i + 1) % count, i) for i in range(ends)]),
            ],
            axis=dim,
        )
    return cells


def layer_norm(values, norm_gain):
    average = jnp.mean(values, axis=-1, keepdims=True)
    centered = values - average
    spread = jnp.mean(centered * centered, axis=-1, keepdims=True)
    return centered * lax.rsqrt(spread + epsilon) * norm_gain


def doc_layout(doc_lengths, first_row, row_total):
    doc_ends = jnp.cumsum(doc_lengths)
    doc_starts = doc_ends - doc_lengths
    doc_total = doc_ends[-1]
    position = first_row + jnp.arange(row_total, dtype=jnp.int32)
    started = doc_starts[None, :] <= position[:, None]
    doc_id = jnp.sum(started.astype(jnp.int32), axis=1) - 1
    start_of = jnp.max(jnp.where(started, doc_starts[None, :], 0), axis=1)
    inside = (position >= 0) & (position < doc_total)
    return (jnp.where(inside, doc_id, -1), position - start_of)


def rotate(values, offsets):
    half_dim = HEAD_DIM // 2
    row_count = values.shape[0]
    head_count = values.shape[1] // HEAD_DIM
    frequency = rope_base ** (-(jnp.arange(half_dim, dtype=jnp.float32) * 2.0) / HEAD_DIM)
    angles = offsets.astype(jnp.float32)[:, None] * frequency[None, :]
    cosine = jnp.cos(angles)[:, None, :]
    sine_part = jnp.sin(angles)[:, None, :]
    shaped = values.reshape(row_count, head_count, HEAD_DIM)
    first_half = shaped[..., :half_dim]
    second_half = shaped[..., half_dim:]
    turned = jnp.concatenate(
        [
            first_half * cosine - second_half * sine_part,
            second_half * cosine + first_half * sine_part,
        ],
        axis=-1,
    )
    return turned.reshape(row_count, head_count * HEAD_DIM)


def project_heads(projected, doc_lengths, first_row):
    inner_width = projected.shape[1] // 3
    _, offsets = doc_layout(doc_lengths, first_row, projected.shape[0])
    queries = rotate(projected[:, :inner_width], offsets).astype(jnp.bfloat16)
    key_part = rotate(projected[:, inner_width : 2 * inner_width], offsets)
    key_value = jnp.concatenate([key_part, projected[:, 2 * inner_width :]], axis=1).astype(
        jnp.bfloat16
    )
    return (queries, key_value)


def attend(queries, padded, doc_lengths, first_row):
    row_count = queries.shape[0]
    inner_width = queries.shape[1]
    head_count = inner_width // HEAD_DIM
    query_docs, _ = doc_layout(doc_lengths, first_row, row_count)
    key_docs, _ = doc_layout(doc_lengths, first_row - WIN, row_count + 2 * WIN)
    block_rows = min(512, row_count)
    key_span = block_rows + 2 * WIN
    outputs = []
    for block_index in range(row_count // block_rows):
        block_low = block_index * block_rows
        query_block = queries[block_low : block_low + block_rows].reshape(
            block_rows, head_count, HEAD_DIM
        )
        key_block = padded[block_low : block_low + key_span, :inner_width].reshape(
            key_span, head_count, HEAD_DIM
        )
        value_block = padded[block_low : block_low + key_span, inner_width:].reshape(
            key_span, head_count, HEAD_DIM
        )
        scores = jnp.einsum(
            "qhd,khd->hqk", query_block, key_block, preferred_element_type=jnp.float32
        ) * HEAD_DIM ** (-0.5)
        key_lag = jnp.arange(key_span)[None, :] - jnp.arange(block_rows)[:, None]
        allowed = (
            (key_lag >= 0)
            & (key_lag <= 2 * WIN)
            & (
                query_docs[block_low : block_low + block_rows, None]
                == key_docs[None, block_low : block_low + key_span]
            )
        )
        scores = jnp.where(allowed[None], scores, -jnp.inf)
        row_max = jnp.max(scores, axis=2, keepdims=True)
        weights = jnp.exp(scores - row_max)
        probabilities = (weights / jnp.sum(weights, axis=2, keepdims=True)).astype(jnp.bfloat16)
        mixed = jnp.einsum(
            "hqk,khd->qhd", probabilities, value_block, preferred_element_type=jnp.float32
        )
        outputs.append(mixed.reshape(block_rows, inner_width))
    return jnp.concatenate(outputs, axis=0).astype(jnp.bfloat16)


def gated_hidden(normed, weight_in, weight_gate):
    gate_in = jnp.dot(normed, weight_in, preferred_element_type=jnp.float32)
    gate_side = jnp.dot(normed, weight_gate, preferred_element_type=jnp.float32)
    return (jax.nn.gelu(gate_in, approximate=False) * gate_side).astype(jnp.bfloat16)


def down_product(hidden, weight_down):
    return lax.dot_general(
        hidden, weight_down, (((1,), (1,)), ((), ())), preferred_element_type=jnp.float32
    )


def per_device(
    tokens,
    w_qkv,
    w_attn_out,
    w_in,
    w_gate,
    w_down,
    w_colbert,
    gain_attn,
    gain_mlp,
    gain_final,
    lengths,
    owners,
):
    row_count = tokens.shape[1]
    model_width = tokens.shape[2]
    doc_lengths = lengths[0]
    local_tokens = tokens[0].astype(jnp.float32)
    normed = layer_norm(local_tokens, gain_attn).astype(jnp.bfloat16)
    seq_index = lax.axis_index("seq")
    mp_size = lax.axis_size("mp")
    first_row = seq_index * (row_count * mp_size)
    local_qkv = w_qkv.reshape(model_width, -1)
    projected = jnp.dot(
        lax.all_gather(normed, "mp", axis=0, tiled=True),
        local_qkv,
        preferred_element_type=jnp.float32,
    )
    queries, key_value = project_heads(projected, doc_lengths, first_row)
    padded = with_halo(key_value, (("seq", 0),), WIN)
    context = attend(queries, padded, doc_lengths, first_row)
    mixed = local_tokens + lax.psum_scatter(
        jnp.dot(context, w_attn_out, preferred_element_type=jnp.float32),
        "mp",
        scatter_dimension=0,
        tiled=True,
    )
    mlp_normed = layer_norm(mixed, gain_mlp).astype(jnp.bfloat16)
    hidden = gated_hidden(lax.all_gather(mlp_normed, "mp", axis=0, tiled=True), w_in, w_gate)
    result = mixed + lax.psum_scatter(
        down_product(hidden, w_down).astype(jnp.bfloat16), "mp", scatter_dimension=0, tiled=True
    ).astype(jnp.float32)
    final_normed = layer_norm(result, gain_final).astype(jnp.bfloat16)
    colbert_raw = jnp.dot(final_normed, w_colbert, preferred_element_type=jnp.float32)
    vectors = (
        colbert_raw * lax.rsqrt(jnp.mean(colbert_raw * colbert_raw, axis=1, keepdims=True) + 1e-06)
    ).astype(jnp.bfloat16)
    owner_ids = owners[0, :, 0]
    seq_size = lax.axis_size("seq")
    peer_count = seq_size * mp_size * lax.axis_size("rep")
    slot_count = max(2, 2 * row_count // peer_count)
    chosen = (owner_ids[:, None] == jnp.arange(peer_count, dtype=jnp.int32)[None, :]).astype(
        jnp.bfloat16
    )
    earlier = (jnp.arange(row_count)[:, None] >= jnp.arange(row_count)[None, :]).astype(
        jnp.bfloat16
    )
    running = jnp.dot(earlier, chosen, preferred_element_type=jnp.float32)
    slot_rank = jnp.sum(running * chosen.astype(jnp.float32), axis=1).astype(jnp.int32) - 1
    target = owner_ids * slot_count + slot_rank
    dispatch = (
        target[None, :] == jnp.arange(peer_count * slot_count, dtype=jnp.int32)[:, None]
    ).astype(jnp.bfloat16)
    outgoing = jnp.dot(dispatch, vectors, preferred_element_type=jnp.float32).astype(jnp.bfloat16)
    outgoing = outgoing.reshape(peer_count, slot_count, -1)
    received = lax.all_to_all(
        outgoing, ("seq", "mp", "rep"), split_axis=0, concat_axis=0, tiled=True
    )
    return received


def solution(mesh):
    return jax.shard_map(
        per_device,
        mesh=mesh,
        in_specs=(
            P(("groups", "rep"), ("seq", "mp"), None),
            P(None, None, "mp"),
            P("mp", None),
            P(None, "mp"),
            P(None, "mp"),
            P(None, "mp"),
            P(),
            P(),
            P(),
            P(),
            P(("groups", "rep"), None),
            P(("groups", "rep"), ("seq", "mp"), None),
        ),
        out_specs=P(("groups", "seq", "mp", "rep"), None, None),
        check_vma=False,
    )
```

profile of v0, /device:TPU:0, one launch (start us, length us, event | category | flops | bytes accessed | tf_op | source)
XLA Modules:
  0.0 203.6 jit_solution(9962105180410192635)
XLA Ops:
  6.5 0.0 copy-start
  6.5 0.0 all-gather.3.cloned.1.call-start
  6.5 1.3 convert_reduce_fusion
  7.9 1.3 fusion.90
  9.2 2.1 %fusion.92 = bf16[256,1024]{1,0:T(8,128)(2,1)} fusion(bf16[1,256,1024]{2,1,0:T(8,128)(2,1)} %param.12, f32[1024]{0:T(1024)} %param.19, f32[256]{0:T(256)S(1)} %add_rsqrt_fusion.3, f32[256]{0:T(256)S(1)} %broadcast_multiply_fusion.2), kind=kLoop, calls=%fused_computation.107 | loop fusion | flops 1310720 | bytes 1054720 | tf_op jit(solution)/shard_map/convert_element_type | solution.py:155
  11.4 0.0 all-gather.3.cloned.1.call-update
  11.4 0.0 reduce-scatter.3.cloned.1.call-start
  11.5 0.8 reduce-window.4
  12.3 0.7 fusion.108
  13.0 0.6 slice.46
  13.5 4.7 %copy.26 = bf16[1024,3,512]{0,2,1:T(8,128)(2,1)} copy(bf16[1024,3,512]{2,0,1:T(8,128)(2,1)} %param.13) | data formatting | bytes 6291456 | tf_op args[1]
  18.2 0.1 fusion.102
  18.3 0.1 convert_reduce_fusion.1
  18.4 0.7 add_select_fusion
  19.1 0.7 add_select_fusion.1
  19.7 0.3 multiply_cosine_fusion
  20.0 15.6 %all-gather.3.cloned.1.call-done = bf16[512,1024]{1,0:T(8,128)(2,1)} async-done(((bf16[256,1024]{1,0:T(8,128)(2,1)}), bf16[512,1024]{1,0:T(8,128)(2,1)}) %all-gather.3.cloned.1.call-update) | async-done | bytes 1048592 | tf_op jit(solution)/shard_map/all_gather | solution.py:161
  35.6 4.0 %fusion.150 = f32[512,1536]{1,0:T(8,128)S(1)} fusion(bf16[512,1024]{1,0:T(8,128)(2,1)} %all-gather.3.cloned.1.call-done, bf16[1024,1536]{0,1:T(8,128)(2,1)} %bitcast.51), kind=kOutput, calls=%fused_computation.201 | convolution fusion | flops 1610612736 | bytes 7340032 | tf_op jit(solution)/shard_map/dot_general | solution.py:160
  39.6 1.5 fusion.147
  41.2 0.1 slice.69
  41.2 2.6 %copy.30 = f32[512,512]{0,1:T(8,128)} copy(f32[512,512]{1,0:T(8,128)} %get-tuple-element.9) | data formatting | bytes 2097152 | tf_op jit(solution)/shard_map/slice | solution.py:74
  43.8 2.6 %copy.27 = f32[512,512]{0,1:T(8,128)} copy(f32[512,512]{1,0:T(8,128)} %get-tuple-element.10) | data formatting | bytes 2097152 | tf_op jit(solution)/shard_map/slice | solution.py:75
  46.4 2.6 %subtract_convert_fusion = (bf16[512,8,32]{0,2,1:T(8,128)(2,1)}, bf16[512,8,32]{0,2,1:T(8,128)(2,1)}, bf16[512,8,32]{0,2,1:T(8,128)(2,1)S(1)}, bf16[512,8,32]{0,2,1:T(8,128)(2,1)S(1)}) fusion(f32[512,8,64]{0,2,1:T(8,128)} %bitcast.49, f32[512,32]{0,1:T(8,128)S(1)} %get-tuple-element.22, f32[512,32]{0,1:T(8,128)S(1)} %get-tuple-element.21, ...), kind=kLoop, calls=%fused_computation.121 | loop fusion | flops 2097152 | bytes 3276800 | tf_op jit(solution)/shard_map/convert
  49.0 0.8 pad_maximum_fusion.1
  49.9 2.0 %copy.28 = bf16[512,512]{1,0:T(8,128)(2,1)} copy(bf16[512,512]{0,1:T(8,128)(2,1)} %bitcast.52) | data formatting | bytes 1048576 | tf_op jit(solution)/shard_map/reshape | solution.py:68
  51.9 0.9 pad_maximum_fusion.10
  52.8 3.4 %collective-permute-start = (bf16[64,1024]{1,0:T(8,128)(2,1)S(1)}, bf16[64,1024]{1,0:T(8,128)(2,1)S(1)}, u32[]{:S(2)}, u32[]{:S(2)}) collective-permute-start(bf16[64,1024]{1,0:T(8,128)(2,1)S(1)} %get-tuple-element.17), channel_id=1, source_target_pairs={{0,4},{4,8},{8,12},{1,5},{5,9},{9,13},{2,6},{6,10},{10,14},{3,7},{... | collective-permute-start | bytes 393224 | tf_op jit(solution)/shard_map/ppermute | solution.py:22
  56.2 1.3 collective-permute-start.1
  57.5 1.0 fusion.83
  58.5 0.5 collective-permute-done
  58.9 4.1 %collective-permute-done.1 = bf16[64,1024]{1,0:T(8,128)(2,1)S(1)} collective-permute-done((bf16[64,1024]{1,0:T(8,128)(2,1)S(1)}, bf16[64,1024]{1,0:T(8,128)(2,1)S(1)}, u32[]{:S(2)}, u32[]{:S(2)}) %collective-permute-start.1) | collective-permute-done | bytes 131104 | tf_op jit(solution)/shard_map/ppermute | solution.py:24
  63.1 1.2 pad_maximum_fusion
  64.3 0.9 fusion.148
  65.2 2.2 %copy.31 = bf16[640,512]{0,1:T(8,128)(2,1)} copy(bf16[640,512]{1,0:T(8,128)(2,1)} %get-tuple-element.11) | data formatting | bytes 1310720 | tf_op jit(solution)/shard_map/slice | solution.py:96
  67.4 1.1 copy.29
  68.5 9.1 %fusion.149 = (f32[8,512]{1,0:T(8,128)S(1)}, f32[8,512,640]{2,1,0:T(8,128)}) fusion(pred[512,640]{1,0:T(8,128)(4,1)} %fusion.83, bf16[640,8,64]{0,2,1:T(8,128)(2,1)} %bitcast.53, bf16[512,8,32]{0,2,1:T(8,128)(2,1)} %get-tuple-element.14, bf16[512,8,32]{0,2,1:T(8,128)(2,1)} %get-tuple-element.13), kind=kOutput, calls=%fused_computation.200 | convolution fusion | flops 347079296 | bytes 12009472 | tf_op jit(solution)/shard_map/sub | solution.py:116
  77.6 0.0 copy-done.6
  77.6 5.9 %fusion.84 = bf16[8,64,512]{2,1,0:T(8,128)(2,1)S(1)} fusion(bf16[640,8,64]{0,2,1:T(8,128)(2,1)S(1)} %bitcast.54, f32[8,512,640]{2,1,0:T(8,128)} %get-tuple-element.24, f32[8,512]{1,0:T(8,128)S(1)} %get-tuple-element.23), kind=kOutput, calls=%fused_computation.98 | convolution fusion | flops 341049344 | bytes 11681792 | tf_op jit(solution)/shard_map/hqk,khd->qhd/dot_general | solution.py:118
  83.5 0.0 copy-done.5
  83.5 0.0 copy-start.3
  83.5 2.1 %fusion.151 = f32[512,1024]{1,0:T(8,128)} fusion(bf16[512,512]{0,1:T(8,128)(2,1)S(1)} %bitcast.55, bf16[512,1024]{1,0:T(8,128)(2,1)S(1)} %copy-done.5), kind=kOutput, calls=%fused_computation.202 | convolution fusion | flops 536870912 | bytes 3670016 | tf_op jit(solution)/shard_map/dot_general | solution.py:169
  85.6 0.0 reduce-scatter.3.cloned.1.call-update
  85.6 0.0 all-gather.5.cloned.1.call-start
  85.6 31.0 %reduce-scatter.3.cloned.1.call-done = f32[256,1024]{1,0:T(8,128)} async-done(((f32[512,1024]{1,0:T(8,128)}), f32[256,1024]{1,0:T(8,128)}) %reduce-scatter.3.cloned.1.call-update) | async-done | bytes 1048592 | tf_op jit(solution)/shard_map/reduce_scatter | solution.py:168
  116.6 0.0 copy-done.3
  116.6 1.4 fusion.145
  118.1 0.2 multiply_reduce_fusion.1
  118.3 0.7 copy-done.1
  119.0 1.0 multiply_convert_fusion.1
  120.0 0.0 all-gather.5.cloned.1.call-update
  120.1 0.2 reduce-scatter.5.cloned.1.call-start
  120.3 21.2 %all-gather.5.cloned.1.call-done = bf16[512,1024]{1,0:T(8,128)(2,1)} async-done(((bf16[256,1024]{1,0:T(8,128)(2,1)}), bf16[512,1024]{1,0:T(8,128)(2,1)}) %all-gather.5.cloned.1.call-update) | async-done | bytes 1048592 | tf_op jit(solution)/shard_map/all_gather | solution.py:175
  141.5 4.3 %fusion.152 = f32[512,1312]{0,1:T(8,128)} fusion(bf16[512,1024]{1,0:T(8,128)(2,1)} %all-gather.5.cloned.1.call-done, bf16[1024,1312]{0,1:T(8,128)(2,1)S(1)} %copy-done), kind=kOutput, calls=%fused_computation.203 | convolution fusion | flops 1375731712 | bytes 6422528 | tf_op jit(solution)/shard_map/dot_general | solution.py:126
  145.9 13.6 %fusion.47 = bf16[512,1024]{1,0:T(8,128)(2,1)} fusion(bf16[1024,1312]{0,1:T(8,128)(2,1)} %param.17, bf16[512,1024]{1,0:T(8,128)(2,1)} %all-gather.5.cloned.1.call-done, bf16[1024,1312]{0,1:T(8,128)(2,1)} %param.16, f32[512,1312]{0,1:T(8,128)} %fusion.152), kind=kOutput, calls=%fused_computation.57 | convolution fusion | flops 2796322816 | bytes 10158080 | tf_op jit(solution)/shard_map/dot_general | solution.py:132
  159.5 0.0 reduce-scatter.5.cloned.1.call-update
  159.5 0.0 copy-done.10
  159.5 0.2 fusion.89
  159.7 20.2 %reduce-scatter.5.cloned.1.call-done = bf16[256,1024]{1,0:T(8,128)(2,1)} async-done(((bf16[512,1024]{1,0:T(8,128)(2,1)}), bf16[256,1024]{1,0:T(8,128)(2,1)}) %reduce-scatter.5.cloned.1.call-update) | async-done | bytes 524304 | tf_op jit(solution)/shard_map/reduce_scatter | solution.py:176
  180.0 1.7 fusion.97
  181.6 1.6 multiply_reduce_fusion
  183.3 0.4 multiply_reduce_fusion.2
  183.7 0.2 convolution_convert_fusion
  184.0 12.5 %all_to_all.5 = bf16[16,32,128]{2,1,0:T(8,128)(2,1)S(1)} all-to-all(bf16[16,32,128]{2,1,0:T(8,128)(2,1)S(1)} %bitcast.56), channel_id=1, replica_groups=mesh['groups'=2,'seq'=4,'mp'=2,'rep'=2] {'seq','mp','rep'}, dimensions={0} | all-to-all | bytes 262144 | tf_op jit(solution)/shard_map/all_to_all | solution.py:202
  196.4 0.7 copy.33
  (26 shorter events, 0.1 us)
Async XLA Ops:
  6.5 135.0 %copy-start = (bf16[1024,1312]{0,1:T(8,128)(2,1)S(1)}, bf16[1024,1312]{0,1:T(8,128)(2,1)}, u32[]{:S(2)}) copy-start(bf16[1024,1312]{0,1:T(8,128)(2,1)} %param.15) | copy-start | bytes 8060932
  6.5 29.1 %all-gather.3.cloned.1.call-start = ((), (), s32[]{:S(2)}) async-start(), calls=%async_computation.3 | async-start | bytes 1572864 | tf_op jit(solution)/shard_map/all_gather | solution.py:161
  11.4 105.2 %reduce-scatter.3.cloned.1.call-start = ((), (), s32[]{:S(2)}) async-start(), calls=%async_computation.4 | async-start | bytes 3145728 | tf_op jit(solution)/shard_map/reduce_scatter | solution.py:168
  52.8 6.1 %collective-permute-start = (bf16[64,1024]{1,0:T(8,128)(2,1)S(1)}, bf16[64,1024]{1,0:T(8,128)(2,1)S(1)}, u32[]{:S(2)}, u32[]{:S(2)}) collective-permute-start(bf16[64,1024]{1,0:T(8,128)(2,1)S(1)} %get-tuple-element.17), channel_id=1, source_target_pairs={{0,4},{4,8},{8,12},{1,5},{5,9},{9,13},{2,6},{6,10},{10,14},{3,7},{... | collective-permute-start | bytes 393224 | tf_op jit(solution)/shard_map/ppermute | solution.py:22
  56.2 6.9 %collective-permute-start.1 = (bf16[64,1024]{1,0:T(8,128)(2,1)S(1)}, bf16[64,1024]{1,0:T(8,128)(2,1)S(1)}, u32[]{:S(2)}, u32[]{:S(2)}) collective-permute-start(bf16[64,1024]{1,0:T(8,128)(2,1)S(1)} %get-tuple-element.18), channel_id=1, source_target_pairs={{4,0},{8,4},{12,8},{5,1},{9,5},{13,9},{6,2},{10,6},{14,10},{7,3},{... | collective-permute-start | bytes 393224 | tf_op jit(solution)/shard_map/ppermute | solution.py:24
  68.5 9.1 %copy-start.6 = (bf16[640,512]{0,1:T(8,128)(2,1)S(1)}, bf16[640,512]{0,1:T(8,128)(2,1)}, u32[]{:S(2)}) copy-start(bf16[640,512]{0,1:T(8,128)(2,1)} %copy.29) | copy-start | bytes 1966084
  77.6 5.9 %copy-start.5 = (bf16[512,1024]{1,0:T(8,128)(2,1)S(1)}, bf16[512,1024]{1,0:T(8,128)(2,1)}, u32[]{:S(2)}) copy-start(bf16[512,1024]{1,0:T(8,128)(2,1)} %param.14) | copy-start | bytes 3145732
  83.5 33.2 %copy-start.3 = (bf16[1,256,1024]{2,1,0:T(8,128)(2,1)S(1)}, bf16[1,256,1024]{2,1,0:T(8,128)(2,1)}, u32[]{:S(2)}) copy-start(bf16[1,256,1024]{2,1,0:T(8,128)(2,1)} %param.12) | copy-start | bytes 1572868
  85.6 33.5 %copy-start.8 = (f32[1024]{0:T(1024)S(1)}, f32[1024]{0:T(1024)}, u32[]{:S(2)}) copy-start(f32[1024]{0:T(1024)} %param.20) | copy-start | bytes 12292
  85.6 55.9 %all-gather.5.cloned.1.call-start = ((), (), s32[]{:S(2)}) async-start(), calls=%async_computation.5 | async-start | bytes 1572864 | tf_op jit(solution)/shard_map/all_gather | solution.py:175
  118.0 1.0 copy-start.1
  120.1 59.9 %reduce-scatter.5.cloned.1.call-start = ((), (), s32[]{:S(2)}) async-start(), calls=%async_computation.6 | async-start | bytes 1572864 | tf_op jit(solution)/shard_map/reduce_scatter | solution.py:176
  145.9 13.6 %copy-start.10 = (s32[1,256,1]{1,2,0:T(1,128)S(1)}, s32[1,256,1]{1,2,0:T(1,128)}, u32[]{:S(2)}) copy-start(s32[1,256,1]{1,2,0:T(1,128)} %param.23) | copy-start | bytes 3076
  159.5 23.8 %copy-start.7 = (bf16[1024,128]{1,0:T(8,128)(2,1)S(1)}, bf16[1024,128]{1,0:T(8,128)(2,1)}, u32[]{:S(2)}) copy-start(bf16[1024,128]{1,0:T(8,128)(2,1)} %param.18) | copy-start | bytes 786436
  159.5 23.8 %copy-start.9 = (f32[1024]{0:T(1024)S(1)}, f32[1024]{0:T(1024)}, u32[]{:S(2)}) copy-start(f32[1024]{0:T(1024)} %param.21) | copy-start | bytes 12292
  180.0 3.3 %copy-start.2 = (f32[256,1024]{1,0:T(8,128)S(1)}, f32[256,1024]{1,0:T(8,128)}, u32[]{:S(2)}) copy-start(f32[256,1024]{1,0:T(8,128)} %copy-done.1) | copy-start | bytes 3145732
  180.0 3.3 %copy-start.4 = (bf16[256,1024]{1,0:T(8,128)(2,1)S(1)}, bf16[256,1024]{1,0:T(8,128)(2,1)}, u32[]{:S(2)}) copy-start(bf16[256,1024]{1,0:T(8,128)(2,1)} %reduce-scatter.5.cloned.1.call-done) | copy-start | bytes 1572868
Sparse Core Ops, SparseCore 0:
  11.5 24.0 all-gather.2
  85.7 30.8 reduce-scatter.2
  120.2 21.2 all-gather.4
  159.6 20.3 reduce-scatter.4
where the time goes:
time: 204 us
  waiting for transfers between devices  92.7 us (45%)
  matrix products  39.9 us (20%)
  other arithmetic  20.6 us (10%)
  local copies, waits for them, and re-layouts  19.7 us (10%)
  between operations  13.3 us (7%)
  blocking collectives  12.5 us (6%)
  starting transfers between devices  5 us (2%)
    reduce_scatter x1, waiting for transfers between devices, per_device(): lax.psum_scatter(jnp.dot(context, w_attn_out, preferred_element_type=jnp....  31 us
    all_gather x1, waiting for transfers between devices, per_device(): lax.all_gather(mlp_normed, 'mp', axis=0, tiled=True)  21.2 us
    reduce_scatter x1, waiting for transfers between devices, per_device(): lax.psum_scatter(down_product(hidden, w_down).astype(jnp.bfloat16), 'mp',...  20.2 us
    all_gather x1, waiting for transfers between devices, per_device(): lax.all_gather(normed, 'mp', axis=0, tiled=True)  15.6 us
    dot_general x1, matrix products, down_product(): lax.dot_general(hidden, weight_down, (((1,), (1,)), ((), ())), preferred_...  13.6 us
    all_to_all x1, blocking collectives, per_device(): lax.all_to_all(outgoing, ('seq', 'mp', 'rep'), split_axis=0, concat_axis=...  12.5 us
    sub x1, matrix products, attend(): weights = jnp.exp(scores - row_max)  9.07 us
    unnamed x24, local copies, waits for them, and re-layouts  6.09 us
  transfers between devices with their start and end apart: 6, of which 6 were waited for; matrix products, arithmetic and copies ran while one was open for 5% of the time, Pallas kernels for 0%

commit v1 on v0

v1 whole, which is shorter than its diff:
```python
import functools

import jax
import jax.numpy as jnp
from jax import lax
from jax.experimental import pallas as pl
from jax.experimental.pallas import tpu as pltpu
from jax.sharding import PartitionSpec as P

HEAD_DIM = 64
WIN = 64
LANES = 128
MESH = pl.DeviceIdType.MESH
EPS = 1e-05
LOG_BASE = 9.210340371976184

CHUNK = 64
BLOCK = 128
COLS = 256

f32 = jnp.float32
bf16 = jnp.bfloat16


def layer_norm(values, gain):
    average = jnp.mean(values, axis=-1, keepdims=True)
    centered = values - average
    spread = jnp.mean(centered * centered, axis=-1, keepdims=True)
    return centered * lax.rsqrt(spread + EPS) * gain


def dot(a, b):
    return jnp.dot(a, b, preferred_element_type=f32)


def dot_nt(a, b):
    return lax.dot_general(a, b, (((1,), (1,)), ((), ())), preferred_element_type=f32)


def layer_kernel(
    sizes,
    lengths,
    tokens,
    owner_row,
    gain_attn,
    gain_mlp,
    gain_final,
    w_colbert,
    w_qkv_hbm,
    w_out_hbm,
    w_in_hbm,
    w_gate_hbm,
    w_down_hbm,
    out,
    w_qkv,
    w_out,
    w_in,
    w_gate,
    w_down,
    xn,
    xn2,
    qkv,
    edge,
    cosine,
    sine,
    disp,
    mixed,
    total,
    rs1s,
    rs1r,
    rs2s,
    rs2r,
    ctx,
    hid,
    vec,
    outb,
    w_sem,
    ag1_s,
    ag1_r,
    halo_s,
    halo_r,
    rs1_ss,
    rs1_rs,
    ag2_s,
    ag2_r,
    rs2_ss,
    rs2_rs,
    a2a_s,
    a2a_r,
    own_sem,
):
    seqs, mps, reps = sizes
    peers = seqs * mps * reps
    rows = tokens.shape[0]
    span = rows * mps
    inner = w_out.shape[0]
    pairs = inner // LANES
    hidden = w_in.shape[0]
    slots = out.shape[1]
    chunks = rows // CHUNK
    blocks = rows // BLOCK

    seq = lax.axis_index("seq")
    mp = lax.axis_index("mp")
    rep = lax.axis_index("rep")
    me = (seq * mps + mp) * reps + rep
    first_row = seq * span

    def device(p):
        return {
            "seq": lax.div(p, mps * reps),
            "mp": lax.rem(lax.div(p, reps), mps),
            "rep": lax.rem(p, reps),
        }

    weights = [
        pltpu.make_async_copy(src, dst, w_sem.at[i])
        for i, (src, dst) in enumerate(
            [
                (w_qkv_hbm, w_qkv),
                (w_out_hbm, w_out),
                (w_in_hbm, w_in),
                (w_gate_hbm, w_gate),
                (w_down_hbm, w_down),
            ]
        )
    ]
    for copy in weights:
        copy.start()

    barrier = pltpu.get_barrier_semaphore()

    @pl.loop(1, peers)
    def _(k):
        pl.semaphore_signal(
            barrier, inc=1, device_id=device(lax.rem(me + k, peers)), device_id_type=MESH
        )

    def mp_copy(src, dst, send, recv, k):
        return pltpu.make_async_remote_copy(
            src_ref=src,
            dst_ref=dst,
            send_sem=send,
            recv_sem=recv,
            device_id={"mp": lax.rem(mp + k, mps)},
            device_id_type=MESH,
        )

    def chunk_row(owner, c):
        last = lax.div(owner, mps - 1)
        return pl.multiple_of((c + last * (chunks - 1 - 2 * c)) * CHUNK, CHUNK)

    def ag1(owner, c, k):
        at = pl.ds(pl.multiple_of(owner * rows + chunk_row(owner, c), CHUNK), CHUNK)
        return mp_copy(xn.at[at], xn.at[at], ag1_s.at[k - 1, c], ag1_r.at[k - 1, c], k)

    for c in range(chunks):
        at = chunk_row(mp, c)
        part = layer_norm(tokens[pl.ds(at, CHUNK), :].astype(f32), gain_attn[...])
        xn[pl.ds(pl.multiple_of(mp * rows + at, CHUNK), CHUNK), :] = part.astype(bf16)
        if c == 0:
            pl.semaphore_wait(barrier, peers - 1)
        for k in range(1, mps):
            ag1(mp, c, k).start()

    docs = lengths.shape[1]
    starts = [jnp.int32(0)]
    for d in range(docs):
        starts.append(starts[-1] + lengths[0, d])

    def doc_bounds(position):
        low = jnp.zeros_like(position)
        high = jnp.zeros_like(position) + starts[1]
        for d in range(1, docs):
            inside = position >= starts[d]
            low = jnp.where(inside, starts[d], low)
            high = jnp.where(inside, starts[d + 1], high)
        return low, high

    lane = lax.broadcasted_iota(jnp.int32, (1, LANES), 1)
    first_half = lax.rem(lane, HEAD_DIM) < HEAD_DIM // 2
    frequency = jnp.exp(
        lax.rem(lane, HEAD_DIM // 2).astype(f32) * (-2.0 * LOG_BASE / HEAD_DIM)
    )

    @pl.loop(0, span // CHUNK)
    def _(i):
        at = pl.ds(pl.multiple_of(i * CHUNK, CHUNK), CHUNK)
        position = first_row + i * CHUNK + lax.broadcasted_iota(jnp.int32, (CHUNK, 1), 0)
        offset = position - doc_bounds(position)[0]
        angle = offset.astype(f32) * frequency
        cosine[at, :] = jnp.cos(angle)
        turned = jnp.sin(angle)
        sine[at, :] = jnp.where(first_half, -turned, turned)

    def rotate(values, c, s):
        swapped = jnp.where(
            first_half,
            pltpu.roll(values, LANES - HEAD_DIM // 2, 1),
            pltpu.roll(values, HEAD_DIM // 2, 1),
        )
        return values * c + swapped * s

    weights[0].wait()

    def project(x, part, c, s, put):
        for low in range(0, inner, COLS):
            y = dot(x, w_qkv[part, :, low : low + COLS])
            for half in range(0, COLS, LANES):
                piece = y[:, half : half + LANES]
                if part < 2:
                    piece = rotate(piece, c, s)
                if part == 0:
                    piece = piece * HEAD_DIM**-0.5
                put(low + half, piece.astype(bf16))

    for k in range(1, mps):
        ag1(lax.rem(mp + mps - k, mps), 0, k).wait_recv()
    top = span - WIN
    x_edge = jnp.concatenate([xn[0:WIN, :], xn[top:span, :]], axis=0)
    c_edge = jnp.concatenate([cosine[0:WIN, :], cosine[top:span, :]], axis=0)
    s_edge = jnp.concatenate([sine[0:WIN, :], sine[top:span, :]], axis=0)
    for part in (1, 2):

        def put_edge(col, piece, base=(part - 1) * inner):
            edge[:, base + col : base + col + LANES] = piece

        project(x_edge, part, c_edge, s_edge, put_edge)

    def halo(side):
        src = edge.at[pl.ds(side * WIN, WIN), :]
        dst = qkv.at[pl.ds((WIN + span) * (1 - side), WIN), pl.ds(inner, 2 * inner)]
        to = lax.rem(seq + (seqs - 1 if side == 0 else 1), seqs)
        return pltpu.make_async_remote_copy(
            src_ref=src,
            dst_ref=dst,
            send_sem=halo_s.at[side],
            recv_sem=halo_r.at[side],
            device_id={"seq": to},
            device_id_type=MESH,
        )

    @pl.when(seq > 0)
    def _():
        halo(0).start()

    @pl.when(seq < seqs - 1)
    def _():
        halo(1).start()

    @pl.when(seq == 0)
    def _():
        qkv[0:WIN, inner:] = jnp.zeros((WIN, 2 * inner), bf16)

    @pl.when(seq == seqs - 1)
    def _():
        qkv[WIN + span :, inner:] = jnp.zeros((WIN, 2 * inner), bf16)

    @pl.loop(0, mps)
    def _(i):
        owner = lax.rem(mp + mps - i, mps)

        @pl.when(i > 0)
        def _():
            for c in range(1, chunks):
                at = pl.ds(pl.multiple_of(owner * rows + chunk_row(owner, c), CHUNK), CHUNK)
                mp_copy(
                    xn.at[at], xn.at[at], ag1_s.at[i - 1, c], ag1_r.at[i - 1, c], i
                ).wait_recv()

        at = pl.multiple_of(owner * rows, rows)
        x = xn[pl.ds(at, rows), :]
        c, s = cosine[pl.ds(at, rows), :], sine[pl.ds(at, rows), :]
        for part in range(3):

            def put(col, piece, base=part * inner):
                qkv[pl.ds(pl.multiple_of(at + WIN, WIN), rows), base + col : base + col + LANES] = piece

            project(x, part, c, s, put)

    owner_of = owner_row[...]
    chosen = (owner_of == lax.broadcasted_iota(jnp.int32, (peers, rows), 0)).astype(f32)
    before = (
        lax.broadcasted_iota(jnp.int32, (rows, rows), 0)
        <= lax.broadcasted_iota(jnp.int32, (rows, rows), 1)
    ).astype(f32)
    running = dot(chosen.astype(bf16), before.astype(bf16))
    rank = jnp.sum(running * chosen, axis=0, keepdims=True) - 1.0
    target = owner_of.astype(f32) * slots + rank
    slot_id = lax.broadcasted_iota(jnp.int32, (peers * slots, rows), 0).astype(f32)
    disp[...] = (target == slot_id).astype(f32).astype(bf16)

    weights[1].wait()

    @pl.when(seq < seqs - 1)
    def _():
        halo(0).wait_recv()

    @pl.when(seq > 0)
    def _():
        halo(1).wait_recv()

    head_lane = lane < HEAD_DIM
    ones = jnp.ones((BLOCK + 2 * WIN, LANES), bf16)

    def attend(low):
        position = first_row + low + lax.broadcasted_iota(jnp.int32, (BLOCK, 1), 0)
        start, end = doc_bounds(position)
        start = jnp.maximum(start, position - WIN)
        end = jnp.minimum(end - 1, position + WIN)
        key = first_row + low - WIN + lax.broadcasted_iota(jnp.int32, (1, BLOCK + 2 * WIN), 1)
        allowed = (key >= start) & (key <= end)
        allowed = jnp.concatenate([allowed.astype(f32)] * 2, axis=0) > 0.5
        at_q = pl.ds(pl.multiple_of(low + WIN, WIN), BLOCK)
        at_k = pl.ds(pl.multiple_of(low, WIN), BLOCK + 2 * WIN)
        for pair in range(pairs):
            col = pair * LANES
            q = qkv[at_q, col : col + LANES].astype(f32)
            q = jnp.concatenate(
                [jnp.where(head_lane, q, 0.0), jnp.where(head_lane, 0.0, q)], axis=0
            ).astype(bf16)
            scores = dot_nt(q, qkv[at_k, inner + col : inner + col + LANES])
            scores = jnp.where(allowed, scores, -jnp.inf)
            weight = jnp.exp(scores - jnp.max(scores, axis=1, keepdims=True)).astype(bf16)
            v = qkv[at_k, 2 * inner + col : 2 * inner + col + LANES]
            o = dot(weight, jnp.concatenate([v, ones], axis=1))
            o = o[:, :LANES] / o[:, LANES:]
            ctx[:, col : col + LANES] = jnp.where(head_lane, o[:BLOCK], o[BLOCK:]).astype(bf16)
        return dot(ctx[...], w_out[...])

    def spread(buffer_s, buffer_r, send, recv, k, b):
        at = pl.ds(pl.multiple_of(b * BLOCK, BLOCK), BLOCK)
        return mp_copy(
            buffer_s.at[k - 1, at], buffer_r.at[k - 1, at], send.at[k - 1, b], recv.at[k - 1, b], k
        )

    @pl.loop(0, mps * blocks)
    def _(i):
        k = 1 + lax.rem(i, mps - 1) if mps > 2 else 1
        b = lax.div(i, mps - 1)
        is_own = i >= (mps - 1) * blocks
        own_b = i - (mps - 1) * blocks
        owner = jnp.where(is_own, mp, lax.rem(mp + k, mps))
        b = jnp.where(is_own, own_b, b)
        partial = attend(owner * rows + b * BLOCK)
        at = pl.ds(pl.multiple_of(b * BLOCK, BLOCK), BLOCK)

        @pl.when(is_own)
        def _():
            mixed[at, :] = partial + tokens[at, :].astype(f32)

        @pl.when(jnp.logical_not(is_own))
        def _():
            rs1s[k - 1, at, :] = partial.astype(bf16)
            spread(rs1s, rs1r, rs1_ss, rs1_rs, k, b).start()

    def ag2(owner, b, k):
        at = pl.ds(pl.multiple_of(owner * rows + b * BLOCK, BLOCK), BLOCK)
        return mp_copy(xn2.at[at], xn2.at[at], ag2_s.at[k - 1, b], ag2_r.at[k - 1, b], k)

    for b in range(blocks):
        at = slice(b * BLOCK, (b + 1) * BLOCK)
        value = mixed[at, :]
        for k in range(1, mps):
            spread(rs1s, rs1r, rs1_ss, rs1_rs, k, b).wait_recv()
            value = value + rs1r[k - 1, at, :].astype(f32)
        mixed[at, :] = value
        low = pl.multiple_of(mp * rows + b * BLOCK, BLOCK)
        xn2[pl.ds(low, BLOCK), :] = layer_norm(value, gain_mlp[...]).astype(bf16)
        for k in range(1, mps):
            ag2(mp, b, k).start()

    for copy in weights[2:]:
        copy.wait()

    def mlp(low):
        x = xn2[pl.ds(pl.multiple_of(low, BLOCK), BLOCK), :]
        for at in range(0, hidden, COLS):
            to = min(at + COLS, hidden)
            a = dot_nt(x, w_in[at:to, :])
            g = dot_nt(x, w_gate[at:to, :])
            a = 0.5 * a * (1.0 + lax.erf(a * (0.5**0.5)))
            hid[:, at:to] = (a * g).astype(bf16)
        return dot(hid[...], w_down[...])

    others = (mps - 1) * blocks

    @pl.loop(0, mps * blocks)
    def _(i):
        j = jnp.clip(i - 1, 0, others - 1)
        is_other = (i >= 1) & (i <= others)
        k = 1 + lax.rem(j, mps - 1) if mps > 2 else 1
        b = jnp.where(is_other, lax.div(j, mps - 1), jnp.maximum(i - others, 0))
        owner = jnp.where(is_other, lax.rem(mp + k, mps), mp)

        @pl.when(is_other)
        def _():
            back = mps - k
            at = pl.ds(pl.multiple_of(owner * rows + b * BLOCK, BLOCK), BLOCK)
            mp_copy(
                xn2.at[at], xn2.at[at], ag2_s.at[back - 1, b], ag2_r.at[back - 1, b], back
            ).wait_recv()

        partial = mlp(owner * rows + b * BLOCK)
        at = pl.ds(pl.multiple_of(b * BLOCK, BLOCK), BLOCK)

        @pl.when(is_other)
        def _():
            rs2s[k - 1, at, :] = partial.astype(bf16)
            spread(rs2s, rs2r, rs2_ss, rs2_rs, k, b).start()

        @pl.when(jnp.logical_not(is_other))
        def _():
            total[at, :] = partial + mixed[at, :]

    for b in range(blocks):
        at = slice(b * BLOCK, (b + 1) * BLOCK)
        value = total[at, :]
        for k in range(1, mps):
            spread(rs2s, rs2r, rs2_ss, rs2_rs, k, b).wait_recv()
            value = value + rs2r[k - 1, at, :].astype(f32)
        final = layer_norm(value, gain_final[...]).astype(bf16)
        raw = dot(final, w_colbert[...])
        vec[at, :] = (
            raw * lax.rsqrt(jnp.mean(raw * raw, axis=1, keepdims=True) + 1e-06)
        ).astype(bf16)

    routed = dot(disp[...], vec[...])
    for p in range(peers):
        outb[p] = routed[p * slots : (p + 1) * slots].astype(bf16)

    def a2a(to, source):
        return pltpu.make_async_remote_copy(
            src_ref=outb.at[to],
            dst_ref=out.at[source],
            send_sem=a2a_s.at[to],
            recv_sem=a2a_r.at[source],
            device_id=device(to),
            device_id_type=MESH,
        )

    @pl.loop(1, peers)
    def _(k):
        a2a(lax.rem(me + k, peers), me).start()

    own = pltpu.make_async_copy(outb.at[me], out.at[me], own_sem)
    own.start()

    for k in range(1, mps):
        for c in range(chunks):
            ag1(mp, c, k).wait_send()
        for b in range(blocks):
            spread(rs1s, rs1r, rs1_ss, rs1_rs, k, b).wait_send()
            ag2(mp, b, k).wait_send()
            spread(rs2s, rs2r, rs2_ss, rs2_rs, k, b).wait_send()

    @pl.when(seq > 0)
    def _():
        halo(0).wait_send()

    @pl.when(seq < seqs - 1)
    def _():
        halo(1).wait_send()

    own.wait()

    @pl.loop(1, peers)
    def _(k):
        other = lax.rem(me + k, peers)
        a2a(other, me).wait_send()
        a2a(other, other).wait_recv()


def per_device(
    sizes,
    tokens,
    w_qkv,
    w_attn_out,
    w_in,
    w_gate,
    w_down,
    w_colbert,
    gain_attn,
    gain_mlp,
    gain_final,
    lengths,
    owners,
):
    seqs, mps, reps = sizes
    rows, width = tokens.shape[1:]
    peers = seqs * mps * reps
    slots = max(2, 2 * rows // peers)
    inner = w_attn_out.shape[0]
    hidden = w_in.shape[1]
    span = rows * mps
    dc = w_colbert.shape[1]
    chunks, blocks = rows // CHUNK, rows // BLOCK
    vmem = pl.BlockSpec(memory_space=pltpu.VMEM)
    anywhere = pl.BlockSpec(memory_space=pl.ANY)
    dma = pltpu.SemaphoreType.DMA
    return pl.pallas_call(
        functools.partial(layer_kernel, sizes),
        out_shape=jax.ShapeDtypeStruct((peers, slots, dc), bf16),
        in_specs=[pl.BlockSpec(memory_space=pltpu.SMEM)] + [vmem] * 6 + [anywhere] * 5,
        out_specs=anywhere,
        scratch_shapes=[
            pltpu.VMEM((3, width, inner), bf16),
            pltpu.VMEM((inner, width), bf16),
            pltpu.VMEM((hidden, width), bf16),
            pltpu.VMEM((hidden, width), bf16),
            pltpu.VMEM((hidden, width), bf16),
            pltpu.VMEM((span, width), bf16),
            pltpu.VMEM((span, width), bf16),
            pltpu.VMEM((span + 2 * WIN, 3 * inner), bf16),
            pltpu.VMEM((2 * WIN, 2 * inner), bf16),
            pltpu.VMEM((span, LANES), f32),
            pltpu.VMEM((span, LANES), f32),
            pltpu.VMEM((peers * slots, rows), bf16),
            pltpu.VMEM((rows, width), f32),
            pltpu.VMEM((rows, width), f32),
            pltpu.VMEM((mps - 1, rows, width), bf16),
            pltpu.VMEM((mps - 1, rows, width), bf16),
            pltpu.VMEM((mps - 1, rows, width), bf16),
            pltpu.VMEM((mps - 1, rows, width), bf16),
            pltpu.VMEM((BLOCK, inner), bf16),
            pltpu.VMEM((BLOCK, hidden), bf16),
            pltpu.VMEM((rows, dc), bf16),
            pltpu.VMEM((peers, slots, dc), bf16),
            dma((5,)),
            dma((mps - 1, chunks)),
            dma((mps - 1, chunks)),
            dma((2,)),
            dma((2,)),
            dma((mps - 1, blocks)),
            dma((mps - 1, blocks)),
            dma((mps - 1, blocks)),
            dma((mps - 1, blocks)),
            dma((mps - 1, blocks)),
            dma((mps - 1, blocks)),
            dma((peers,)),
            dma((peers,)),
            dma,
        ],
        compiler_params=pltpu.CompilerParams(
            collective_id=0, has_side_effects=True, vmem_limit_bytes=48 * 1024 * 1024
        ),
    )(
        lengths,
        tokens[0],
        owners.reshape(1, rows),
        gain_attn.reshape(1, width),
        gain_mlp.reshape(1, width),
        gain_final.reshape(1, width),
        w_colbert,
        jnp.transpose(w_qkv, (1, 0, 2)),
        w_attn_out,
        w_in.T,
        w_gate.T,
        w_down.T,
    )


def solution(mesh):
    sizes = (mesh.shape["seq"], mesh.shape["mp"], mesh.shape["rep"])
    return jax.shard_map(
        functools.partial(per_device, sizes),
        mesh=mesh,
        in_specs=(
            P(("groups", "rep"), ("seq", "mp"), None),
            P(None, None, "mp"),
            P("mp", None),
            P(None, "mp"),
            P(None, "mp"),
            P(None, "mp"),
            P(),
            P(),
            P(),
            P(),
            P(("groups", "rep"), None),
            P(("groups", "rep"), ("seq", "mp"), None),
        ),
        out_specs=P(("groups", "seq", "mp", "rep"), None, None),
        check_vma=False,
    )
```

time: 204 us -> 71.1 us (0.35)
  waiting for transfers between devices: 92.7 us -> 0 us
  Pallas kernels: 0 us -> 61.7 us
  matrix products: 39.9 us -> 0 us
  other arithmetic: 20.6 us -> 0 us
  between operations: 13.3 us -> 0.02 us
  blocking collectives: 12.5 us -> 0 us
  local copies, waits for them, and re-layouts: 19.7 us -> 9.02 us
  starting transfers between devices: 5 us -> 0 us
    pallas_call x0 -> x1, Pallas kernels: none -> 61.7 us  [per_device(): pl.pallas_call(functools.partial(layer_kernel, sizes), out_shape=jax.Shap...]
    reduce_scatter x2 -> x0, waiting for transfers between devices: 51.2 us -> none  [the longest x1 31 us: per_device(): lax.psum_scatter(jnp.dot(context, w_attn_out, preferred_element_type=jnp....]
    all_gather x2 -> x0, waiting for transfers between devices: 36.8 us -> none  [the longest x1 21.2 us: per_device(): lax.all_gather(mlp_normed, 'mp', axis=0, tiled=True)]
    dot_general x8 -> x0, matrix products: 30.8 us -> none  [the longest x1 13.6 us: down_product(): lax.dot_general(hidden, weight_down, (((1,), (1,)), ((), ())), preferred_...]
    all_to_all x1 -> x0, blocking collectives: 12.5 us -> none  [per_device(): lax.all_to_all(outgoing, ('seq', 'mp', 'rep'), split_axis=0, concat_axis=...]
    slice x8 -> x0, local copies, waits for them, and re-layouts: 11.5 us -> none  [the longest x2 4.08 us: project_heads(): queries = rotate(projected[:, :inner_width], offsets).astype(jnp.bfloat16)]
    sub x1 -> x0, matrix products: 9.07 us -> none  [attend(): weights = jnp.exp(scores - row_max)]
    reduce_sum x8 -> x0, other arithmetic: 7.77 us -> none  [the longest x3 4.4 us: layer_norm(): average = jnp.mean(values, axis=-1, keepdims=True)]
  transfers between devices with their start and end apart: 6 -> 0, of which waited for: 6 -> 0; matrix products, arithmetic and copies ran while one was open for 5% -> 0% of each run, Pallas kernels for 0% -> 0%
where the time goes in v1:
time: 71.1 us; the launch traced here: 70.7 us
  Pallas kernels  61.7 us (87%)
  local copies, waits for them, and re-layouts  9.02 us (13%)
    pallas_call x1, Pallas kernels, per_device(): pl.pallas_call(functools.partial(layer_kernel, sizes), out_shape=jax.Shap...  61.7 us
    unnamed x19, local copies, waits for them, and re-layouts  9.02 us

profile of v1, /device:TPU:0, one launch (start us, length us, event | category | flops | bytes accessed | tf_op | source)
XLA Modules:
  0.0 70.7 jit_solution(9598482023064405762)
XLA Ops:
  0.0 0.0 copy-start
  0.0 1.8 %copy-done = bf16[1024,1312]{0,1:T(8,128)(2,1)S(1)} copy-done((bf16[1024,1312]{0,1:T(8,128)(2,1)S(1)}, bf16[1024,1312]{0,1:T(8,128)(2,1)}, u32[]{:S(2)}) %copy-start) | copy-done | bytes 2687000
  1.8 0.0 copy-start.1
  1.8 1.2 %copy-done.1 = bf16[512,1024]{1,0:T(8,128)(2,1)S(1)} copy-done((bf16[512,1024]{1,0:T(8,128)(2,1)S(1)}, bf16[512,1024]{1,0:T(8,128)(2,1)}, u32[]{:S(2)}) %copy-start.1) | copy-done | bytes 1048600
  3.0 0.0 copy-start.2
  3.0 1.0 %copy-done.2 = bf16[1,256,1024]{2,1,0:T(8,128)(2,1)S(1)} copy-done((bf16[1,256,1024]{2,1,0:T(8,128)(2,1)S(1)}, bf16[1,256,1024]{2,1,0:T(8,128)(2,1)}, u32[]{:S(2)}) %copy-start.2) | copy-done | bytes 524312
  4.0 0.0 copy-start.3
  4.0 0.9 %copy-done.3 = bf16[1024,128]{1,0:T(8,128)(2,1)S(1)} copy-done((bf16[1024,128]{1,0:T(8,128)(2,1)S(1)}, bf16[1024,128]{1,0:T(8,128)(2,1)}, u32[]{:S(2)}) %copy-start.3) | copy-done | bytes 262168
  5.0 0.0 copy-start.4
  5.0 0.7 copy-done.4
  5.7 0.0 copy-start.5
  5.7 0.7 copy-done.5
  6.4 0.0 copy-start.6
  6.4 0.7 copy-done.6
  7.0 0.0 copy-start.7
  7.0 0.7 copy-done.7
  7.7 0.0 copy-start.8
  7.7 0.7 copy-done.8
  8.4 61.7 %shard_map.118 = bf16[16,32,128]{2,1,0:T(8,128)(2,1)S(1)} custom-call(s32[1,8]{1,0:T(1,128)S(1)} %copy-done.8, bf16[256,1024]{1,0:T(8,128)(2,1)S(1)} %bitcast.10, s32[1,256]{1,0:T(1,128)S(1)} %bitcast.14, f32[1,1024]{1,0:T(1,128)S(1)} %bitcast.11, f32[1,1024]{1,0:T(1,128)S(1)} %bitcast.12, f32[1,1024]{1,0:T(1,128)S(1)} %bitcast.13, ...), custom_call_target="tpu_custom_call" | custom-call | tf_op jit(solution)/shard_map/pallas_call | solution.py:501
  70.1 0.7 copy.14
Async XLA Ops:
  0.0 1.8 %copy-start = (bf16[1024,1312]{0,1:T(8,128)(2,1)S(1)}, bf16[1024,1312]{0,1:T(8,128)(2,1)}, u32[]{:S(2)}) copy-start(bf16[1024,1312]{0,1:T(8,128)(2,1)} %param.15) | copy-start | bytes 8060932
  1.8 1.2 %copy-start.1 = (bf16[512,1024]{1,0:T(8,128)(2,1)S(1)}, bf16[512,1024]{1,0:T(8,128)(2,1)}, u32[]{:S(2)}) copy-start(bf16[512,1024]{1,0:T(8,128)(2,1)} %w_out_hbm.1) | copy-start | bytes 3145732
  3.0 1.0 %copy-start.2 = (bf16[1,256,1024]{2,1,0:T(8,128)(2,1)S(1)}, bf16[1,256,1024]{2,1,0:T(8,128)(2,1)}, u32[]{:S(2)}) copy-start(bf16[1,256,1024]{2,1,0:T(8,128)(2,1)} %param.12) | copy-start | bytes 1572868
  4.0 0.9 %copy-start.3 = (bf16[1024,128]{1,0:T(8,128)(2,1)S(1)}, bf16[1024,128]{1,0:T(8,128)(2,1)}, u32[]{:S(2)}) copy-start(bf16[1024,128]{1,0:T(8,128)(2,1)} %w_colbert.1) | copy-start | bytes 786436
  5.0 0.7 copy-start.4
  5.7 0.7 copy-start.5
  6.4 0.7 copy-start.6
  7.0 0.7 copy-start.7
  7.7 0.7 copy-start.8

commit v2 on v1

--- a/solution.py
+++ b/solution.py
@@ -39,6 +39,19 @@
 
 def layer_kernel(
     sizes,
+    lengths_hbm,
+    tokens_hbm,
+    owner_row_hbm,
+    gain_attn_hbm,
+    gain_mlp_hbm,
+    gain_final_hbm,
+    w_colbert_hbm,
+    w_qkv_hbm,
+    w_out_hbm,
+    w_in_hbm,
+    w_gate_hbm,
+    w_down_hbm,
+    out,
     lengths,
     tokens,
     owner_row,
@@ -46,12 +59,6 @@
     gain_mlp,
     gain_final,
     w_colbert,
-    w_qkv_hbm,
-    w_out_hbm,
-    w_in_hbm,
-    w_gate_hbm,
-    w_down_hbm,
-    out,
     w_qkv,
     w_out,
     w_in,
@@ -117,7 +124,14 @@
         pltpu.make_async_copy(src, dst, w_sem.at[i])
         for i, (src, dst) in enumerate(
             [
+                (tokens_hbm, tokens),
+                (gain_attn_hbm, gain_attn),
+                (lengths_hbm, lengths),
                 (w_qkv_hbm, w_qkv),
+                (owner_row_hbm, owner_row),
+                (gain_mlp_hbm, gain_mlp),
+                (gain_final_hbm, gain_final),
+                (w_colbert_hbm, w_colbert),
                 (w_out_hbm, w_out),
                 (w_in_hbm, w_in),
                 (w_gate_hbm, w_gate),
@@ -154,6 +168,9 @@
         at = pl.ds(pl.multiple_of(owner * rows + chunk_row(owner, c), CHUNK), CHUNK)
         return mp_copy(xn.at[at], xn.at[at], ag1_s.at[k - 1, c], ag1_r.at[k - 1, c], k)
 
+    for copy in weights[:2]:
+        copy.wait()
+
     for c in range(chunks):
         at = chunk_row(mp, c)
         part = layer_norm(tokens[pl.ds(at, CHUNK), :].astype(f32), gain_attn[...])
@@ -163,6 +180,7 @@
         for k in range(1, mps):
             ag1(mp, c, k).start()
 
+    weights[2].wait()
     docs = lengths.shape[1]
     starts = [jnp.int32(0)]
     for d in range(docs):
@@ -201,7 +219,7 @@
         )
         return values * c + swapped * s
 
-    weights[0].wait()
+    weights[3].wait()
 
     def project(x, part, c, s, put):
         for low in range(0, inner, COLS):
@@ -278,6 +296,8 @@
 
             project(x, part, c, s, put)
 
+    for copy in weights[4:8]:
+        copy.wait()
     owner_of = owner_row[...]
     chosen = (owner_of == lax.broadcasted_iota(jnp.int32, (peers, rows), 0)).astype(f32)
     before = (
@@ -290,7 +310,7 @@
     slot_id = lax.broadcasted_iota(jnp.int32, (peers * slots, rows), 0).astype(f32)
     disp[...] = (target == slot_id).astype(f32).astype(bf16)
 
-    weights[1].wait()
+    weights[8].wait()
 
     @pl.when(seq < seqs - 1)
     def _():
@@ -370,7 +390,7 @@
         for k in range(1, mps):
             ag2(mp, b, k).start()
 
-    for copy in weights[2:]:
+    for copy in weights[9:]:
         copy.wait()
 
     def mlp(low):
@@ -495,15 +515,21 @@
     span = rows * mps
     dc = w_colbert.shape[1]
     chunks, blocks = rows // CHUNK, rows // BLOCK
-    vmem = pl.BlockSpec(memory_space=pltpu.VMEM)
-    anywhere = pl.BlockSpec(memory_space=pl.ANY)
+    anywhere = pl.BlockSpec(memory_space=pltpu.HBM)
     dma = pltpu.SemaphoreType.DMA
     return pl.pallas_call(
         functools.partial(layer_kernel, sizes),
         out_shape=jax.ShapeDtypeStruct((peers, slots, dc), bf16),
-        in_specs=[pl.BlockSpec(memory_space=pltpu.SMEM)] + [vmem] * 6 + [anywhere] * 5,
+        in_specs=[anywhere] * 12,
         out_specs=anywhere,
         scratch_shapes=[
+            pltpu.SMEM(lengths.shape, jnp.int32),
+            pltpu.VMEM((rows, width), bf16),
+            pltpu.VMEM((1, rows), jnp.int32),
+            pltpu.VMEM((1, width), f32),
+            pltpu.VMEM((1, width), f32),
+            pltpu.VMEM((1, width), f32),
+            pltpu.VMEM((width, dc), bf16),
             pltpu.VMEM((3, width, inner), bf16),
             pltpu.VMEM((inner, width), bf16),
             pltpu.VMEM((hidden, width), bf16),
@@ -526,7 +552,7 @@
             pltpu.VMEM((BLOCK, hidden), bf16),
             pltpu.VMEM((rows, dc), bf16),
             pltpu.VMEM((peers, slots, dc), bf16),
-            dma((5,)),
+            dma((12,)),
             dma((mps - 1, chunks)),
             dma((mps - 1, chunks)),
             dma((2,)),
@@ -542,7 +568,7 @@
             dma,
         ],
         compiler_params=pltpu.CompilerParams(
-            collective_id=0, has_side_effects=True, vmem_limit_bytes=48 * 1024 * 1024
+            collective_id=0, has_side_effects=True, vmem_limit_bytes=60 * 1024 * 1024
         ),
     )(
         lengths,

time: 71.1 us -> 63 us (0.89)
  local copies, waits for them, and re-layouts: 9.02 us -> 1.57 us
    unnamed x19 -> x1, local copies, waits for them, and re-layouts: 9.02 us -> 1.57 us
where the time goes in v2:
time: 63 us; the launch traced here: 62.9 us
  Pallas kernels  61.3 us (97%)
  local copies, waits for them, and re-layouts  1.57 us (2%)
    pallas_call x1, Pallas kernels, per_device(): pl.pallas_call(functools.partial(layer_kernel, sizes), out_shape=jax.Shap...  61.3 us
    unnamed x1, local copies, waits for them, and re-layouts  1.57 us

profile of v2, /device:TPU:0, one launch (start us, length us, event | category | flops | bytes accessed | tf_op | source)
XLA Modules:
  0.0 62.9 jit_solution(5128206592762937370)
XLA Ops:
  0.0 61.3 %shard_map.118 = bf16[16,32,128]{2,1,0:T(8,128)(2,1)} custom-call(s32[1,8]{1,0:T(1,128)} %lengths_hbm.1, bf16[256,1024]{1,0:T(8,128)(2,1)} %bitcast.13, s32[1,256]{1,0:T(1,128)} %bitcast.17, f32[1,1024]{1,0:T(1,128)} %bitcast.14, f32[1,1024]{1,0:T(1,128)} %bitcast.15, f32[1,1024]{1,0:T(1,128)} %bitcast.16, bf16[1024,128]{1,0:T(8,128)(2,1)} %w_colbert_hbm.1, ...), custom_call_target="tpu_custom_call" | custom-call | tf_op jit(solution)/shard_map/pallas_call | solution.py:520
  61.3 1.6 %copy.14 = bf16[16,32,128]{2,1,0:T(8,128)(2,1)} copy(bf16[16,32,128]{2,1,0:T(8,128)(2,1)} %shard_map.118) | data formatting | bytes 262144

commit v3 on v2

--- a/solution.py
+++ b/solution.py
@@ -14,7 +14,7 @@
 EPS = 1e-05
 LOG_BASE = 9.210340371976184
 
-CHUNK = 64
+CHUNK = 128
 BLOCK = 128
 COLS = 256
 
@@ -211,91 +211,6 @@
         turned = jnp.sin(angle)
         sine[at, :] = jnp.where(first_half, -turned, turned)
 
-    def rotate(values, c, s):
-        swapped = jnp.where(
-            first_half,
-            pltpu.roll(values, LANES - HEAD_DIM // 2, 1),
-            pltpu.roll(values, HEAD_DIM // 2, 1),
-        )
-        return values * c + swapped * s
-
-    weights[3].wait()
-
-    def project(x, part, c, s, put):
-        for low in range(0, inner, COLS):
-            y = dot(x, w_qkv[part, :, low : low + COLS])
-            for half in range(0, COLS, LANES):
-                piece = y[:, half : half + LANES]
-                if part < 2:
-                    piece = rotate(piece, c, s)
-                if part == 0:
-                    piece = piece * HEAD_DIM**-0.5
-                put(low + half, piece.astype(bf16))
-
-    for k in range(1, mps):
-        ag1(lax.rem(mp + mps - k, mps), 0, k).wait_recv()
-    top = span - WIN
-    x_edge = jnp.concatenate([xn[0:WIN, :], xn[top:span, :]], axis=0)
-    c_edge = jnp.concatenate([cosine[0:WIN, :], cosine[top:span, :]], axis=0)
-    s_edge = jnp.concatenate([sine[0:WIN, :], sine[top:span, :]], axis=0)
-    for part in (1, 2):
-
-        def put_edge(col, piece, base=(part - 1) * inner):
-            edge[:, base + col : base + col + LANES] = piece
-
-        project(x_edge, part, c_edge, s_edge, put_edge)
-
-    def halo(side):
-        src = edge.at[pl.ds(side * WIN, WIN), :]
-        dst = qkv.at[pl.ds((WIN + span) * (1 - side), WIN), pl.ds(inner, 2 * inner)]
-        to = lax.rem(seq + (seqs - 1 if side == 0 else 1), seqs)
-        return pltpu.make_async_remote_copy(
-            src_ref=src,
-            dst_ref=dst,
-            send_sem=halo_s.at[side],
-            recv_sem=halo_r.at[side],
-            device_id={"seq": to},
-            device_id_type=MESH,
-        )
-
-    @pl.when(seq > 0)
-    def _():
-        halo(0).start()
-
-    @pl.when(seq < seqs - 1)
-    def _():
-        halo(1).start()
-
-    @pl.when(seq == 0)
-    def _():
-        qkv[0:WIN, inner:] = jnp.zeros((WIN, 2 * inner), bf16)
-
-    @pl.when(seq == seqs - 1)
-    def _():
-        qkv[WIN + span :, inner:] = jnp.zeros((WIN, 2 * inner), bf16)
-
-    @pl.loop(0, mps)
-    def _(i):
-        owner = lax.rem(mp + mps - i, mps)
-
-        @pl.when(i > 0)
-        def _():
-            for c in range(1, chunks):
-                at = pl.ds(pl.multiple_of(owner * rows + chunk_row(owner, c), CHUNK), CHUNK)
-                mp_copy(
-                    xn.at[at], xn.at[at], ag1_s.at[i - 1, c], ag1_r.at[i - 1, c], i
-                ).wait_recv()
-
-        at = pl.multiple_of(owner * rows, rows)
-        x = xn[pl.ds(at, rows), :]
-        c, s = cosine[pl.ds(at, rows), :], sine[pl.ds(at, rows), :]
-        for part in range(3):
-
-            def put(col, piece, base=part * inner):
-                qkv[pl.ds(pl.multiple_of(at + WIN, WIN), rows), base + col : base + col + LANES] = piece
-
-            project(x, part, c, s, put)
-
     for copy in weights[4:8]:
         copy.wait()
     owner_of = owner_row[...]
@@ -309,6 +224,89 @@
     target = owner_of.astype(f32) * slots + rank
     slot_id = lax.broadcasted_iota(jnp.int32, (peers * slots, rows), 0).astype(f32)
     disp[...] = (target == slot_id).astype(f32).astype(bf16)
+
+    def rotate(values, c, s):
+        swapped = jnp.where(
+            first_half,
+            pltpu.roll(values, LANES - HEAD_DIM // 2, 1),
+            pltpu.roll(values, HEAD_DIM // 2, 1),
+        )
+        return values * c + swapped * s
+
+    weights[3].wait()
+
+    def project(x, part, c, s, put):
+        for low in range(0, inner, COLS):
+            y = dot(x, w_qkv[part, :, low : low + COLS])
+            for half in range(0, COLS, LANES):
+                piece = y[:, half : half + LANES]
+                if part < 2:
+                    piece = rotate(piece, c, s)
+                if part == 0:
+                    piece = piece * HEAD_DIM**-0.5
+                put(low + half, piece.astype(bf16))
+
+    for k in range(1, mps):
+        ag1(lax.rem(mp + mps - k, mps), 0, k).wait_recv()
+    top = span - WIN
+    x_edge = jnp.concatenate([xn[0:WIN, :], xn[top:span, :]], axis=0)
+    c_edge = jnp.concatenate([cosine[0:WIN, :], cosine[top:span, :]], axis=0)
+    s_edge = jnp.concatenate([sine[0:WIN, :], sine[top:span, :]], axis=0)
+    for part in (1, 2):
+
+        def put_edge(col, piece, base=(part - 1) * inner):
+            edge[:, base + col : base + col + LANES] = piece
+
+        project(x_edge, part, c_edge, s_edge, put_edge)
+
+    def halo(side):
+        src = edge.at[pl.ds(side * WIN, WIN), :]
+        dst = qkv.at[pl.ds((WIN + span) * (1 - side), WIN), pl.ds(inner, 2 * inner)]
+        to = lax.rem(seq + (seqs - 1 if side == 0 else 1), seqs)
+        return pltpu.make_async_remote_copy(
+            src_ref=src,
+            dst_ref=dst,
+            send_sem=halo_s.at[side],
+            recv_sem=halo_r.at[side],
+            device_id={"seq": to},
+            device_id_type=MESH,
+        )
+
+    @pl.when(seq > 0)
+    def _():
+        halo(0).start()
+
+    @pl.when(seq < seqs - 1)
+    def _():
+        halo(1).start()
+
+    @pl.when(seq == 0)
+    def _():
+        qkv[0:WIN, inner:] = jnp.zeros((WIN, 2 * inner), bf16)
+
+    @pl.when(seq == seqs - 1)
+    def _():
+        qkv[WIN + span :, inner:] = jnp.zeros((WIN, 2 * inner), bf16)
+
+    @pl.loop(0, mps * chunks)
+    def _(j):
+        i, c = lax.div(j, chunks), lax.rem(j, chunks)
+        owner = lax.rem(mp + mps - i, mps)
+        at = pl.multiple_of(owner * rows + chunk_row(owner, c), CHUNK)
+
+        @pl.when((i > 0) & (c > 0))
+        def _():
+            chunk = xn.at[pl.ds(at, CHUNK)]
+            mp_copy(chunk, chunk, ag1_s.at[i - 1, c], ag1_r.at[i - 1, c], i).wait_recv()
+
+        x = xn[pl.ds(at, CHUNK), :]
+        cos_part, sin_part = cosine[pl.ds(at, CHUNK), :], sine[pl.ds(at, CHUNK), :]
+        for part in range(3):
+
+            def put(col, piece, base=part * inner):
+                qkv[pl.ds(pl.multiple_of(at + WIN, WIN), CHUNK), base + col : base + col + LANES] = piece
+
+            project(x, part, cos_part, sin_part, put)
 
     weights[8].wait()
 

time: 63 us -> 62 us (0.984)
  Pallas kernels: 61.3 us -> 60.3 us
    pallas_call x1, Pallas kernels: 61.3 us -> 60.3 us  [per_device(): pl.pallas_call(functools.partial(layer_kernel, sizes), out_shape=jax.Shap...]
where the time goes in v3:
time: 62 us; the launch traced here: 61.9 us
  Pallas kernels  60.3 us (97%)
  local copies, waits for them, and re-layouts  1.57 us (3%)
    pallas_call x1, Pallas kernels, per_device(): pl.pallas_call(functools.partial(layer_kernel, sizes), out_shape=jax.Shap...  60.3 us
    unnamed x1, local copies, waits for them, and re-layouts  1.57 us

profile of v3, /device:TPU:0, one launch (start us, length us, event | category | flops | bytes accessed | tf_op | source)
XLA Modules:
  0.0 61.9 jit_solution(2652440835738627520)
XLA Ops:
  0.0 60.3 %shard_map.118 = bf16[16,32,128]{2,1,0:T(8,128)(2,1)} custom-call(s32[1,8]{1,0:T(1,128)} %lengths_hbm.1, bf16[256,1024]{1,0:T(8,128)(2,1)} %bitcast.13, s32[1,256]{1,0:T(1,128)} %bitcast.17, f32[1,1024]{1,0:T(1,128)} %bitcast.14, f32[1,1024]{1,0:T(1,128)} %bitcast.15, f32[1,1024]{1,0:T(1,128)} %bitcast.16, bf16[1024,128]{1,0:T(8,128)(2,1)} %w_colbert_hbm.1, ...), custom_call_target="tpu_custom_call" | custom-call | tf_op jit(solution)/shard_map/pallas_call | solution.py:518
  60.3 1.6 %copy.14 = bf16[16,32,128]{2,1,0:T(8,128)(2,1)} copy(bf16[16,32,128]{2,1,0:T(8,128)(2,1)} %shard_map.118) | data formatting | bytes 262144
